TPU v7x, 512 devices: a whole 4x4x16 slice. The times are simulated.
512 devices in a mesh: gx: 8 (over y, core), yz: 64 (over x, z).
Axes of the slice: x: 4, y: 4, z: 16, core: 2. Of those that a mesh axis runs over, the one named last changes fastest.
Arguments:
- right_side: float32 [128, 2048, 128], P('gx', 'yz'), may hold values from -6 to 6
- coefficient: float32 [128, 2048, 128], P('gx', 'yz'), may hold values from 0.5 to 8
Outputs:
- solution: float32 [128, 2048, 128], P('gx', 'yz')
All inputs are finite; a program needn't handle non-finite values.
Results may differ from a plain program's by a relative error of at most 0.0001.
Values sent between devices are 32-bit elements; how exact they have to be, the bound alone decides.
A program may use at most 64 MiB of HBM per device.

v0:
```python
import jax
import jax.numpy as jnp
from jax import lax
from jax.sharding import PartitionSpec as P

LEVELS = 4
BITERS = 4
RELAXATION = 0.8


def padded_2(cells, sides, width):
    for axis, dim in sides:
        count = lax.axis_size(axis)
        ends = count - 1
        head = lax.slice_in_dim(cells, 0, width, axis=dim)
        tail = lax.slice_in_dim(cells, cells.shape[dim] - width, cells.shape[dim], axis=dim)
        cells = jnp.concatenate(
            [
                lax.ppermute(tail, axis, [(i, (i + 1) % count) for i in range(ends)]),
                cells,
                lax.ppermute(head, axis, [((i + 1) % count, i) for i in range(ends)]),
            ],
            axis=dim,
        )
    return cells


def neighbours(padded):
    return [
        padded[2:, 1:-1, 1:-1],
        padded[:-2, 1:-1, 1:-1],
        padded[1:-1, 2:, 1:-1],
        padded[1:-1, :-2, 1:-1],
        padded[1:-1, 1:-1, 2:],
        padded[1:-1, 1:-1, :-2],
    ]


def face_weights(padded):
    centre = padded[1:-1, 1:-1, 1:-1]
    return [0.5 * (centre + other) for other in neighbours(padded)]


def diagonal_of(face_list, level_scale):
    summed = face_list[0]
    for weight in face_list[1:]:
        summed = summed + weight
    return level_scale * summed


def operate(padded, face_list, level_scale):
    centre = padded[1:-1, 1:-1, 1:-1]
    others = neighbours(padded)
    summed = face_list[0] * (centre - others[0])
    for position in range(1, 6):
        summed = summed + face_list[position] * (centre - others[position])
    return level_scale * summed


def restrict(values):
    return values.reshape(
        values.shape[0] // 2, 2, values.shape[1] // 2, 2, values.shape[2] // 2, 2
    ).mean(axis=(1, 3, 5))


def prolong(values):
    return jnp.repeat(jnp.repeat(jnp.repeat(values, 2, 0), 2, 1), 2, 2)


def padded_box(values):
    framed = padded_2(values, (("gx", 0), ("yz", 1)), 1)
    return jnp.pad(framed, ((0, 0), (0, 0), (1, 1)))


def padded_slab(values):
    framed = padded_2(values, (("gx", 0),), 1)
    return jnp.pad(framed, ((0, 0), (1, 1), (1, 1)))


def stabilized_solve(source, weight):
    level_scale = 0.25**LEVELS
    face_list = face_weights(padded_slab(weight))

    def apply_op(values):
        return operate(padded_slab(values), face_list, level_scale)

    answer = jnp.zeros_like(source)
    residual = source
    rho_now = lax.psum(jnp.sum(source * residual), "gx")
    rho_prev = rho_now
    direction = residual
    applied = jnp.zeros_like(source)
    step_alpha = jnp.float32(1.0)
    step_omega = jnp.float32(1.0)
    for turn_index in range(BITERS):
        if turn_index > 0:
            beta_factor = rho_now / rho_prev * (step_alpha / step_omega)
            direction = residual + beta_factor * (direction - step_omega * applied)
        applied = apply_op(direction)
        step_alpha = rho_now / lax.psum(jnp.sum(source * applied), "gx")
        middle = residual - step_alpha * applied
        bent_image = apply_op(middle)
        pair_sums = lax.psum((jnp.sum(bent_image * middle), jnp.sum(bent_image * bent_image)), "gx")
        step_omega = pair_sums[0] / pair_sums[1]
        answer = answer + step_alpha * direction + step_omega * middle
        residual = middle - step_omega * bent_image
        if turn_index + 1 < BITERS:
            rho_prev = rho_now
            rho_now = lax.psum(jnp.sum(source * residual), "gx")
    return answer


def per_device(right_side, coefficient):
    source = right_side
    weight = coefficient
    stored = []
    for level_index in range(LEVELS):
        merged = False
        level_scale = 0.25**level_index
        padder = padded_box
        face_list = face_weights(padder(weight))
        diagonal = diagonal_of(face_list, level_scale)
        iterate = RELAXATION * source / diagonal
        iterate = (
            iterate
            + RELAXATION * (source - operate(padder(iterate), face_list, level_scale)) / diagonal
        )
        residual = source - operate(padder(iterate), face_list, level_scale)
        stored.append((source, iterate, face_list, diagonal, merged))
        if level_index == LEVELS - 1:
            residual, weight = (
                lax.all_gather(residual, "yz", axis=1, tiled=True),
                lax.all_gather(weight, "yz", axis=1, tiled=True),
            )
        source = restrict(residual)
        weight = restrict(weight)
    correction = stabilized_solve(source, weight)
    for level_index in reversed(range(LEVELS)):
        source, iterate, face_list, diagonal, merged = stored[level_index]
        level_scale = 0.25**level_index
        padder = padded_box
        widened = prolong(correction)
        if widened.shape[1] != iterate.shape[1]:
            own_rows = iterate.shape[1]
            widened = lax.dynamic_slice_in_dim(
                widened, lax.axis_index("yz") * own_rows, own_rows, 1
            )
        iterate = iterate + widened
        iterate = (
            iterate
            + RELAXATION * (source - operate(padder(iterate), face_list, level_scale)) / diagonal
        )
        correction = iterate
    return correction


def solution(mesh):
    return jax.shard_map(
        per_device,
        mesh=mesh,
        in_specs=(P("gx", "yz", None), P("gx", "yz", None)),
        out_specs=P("gx", "yz", None),
        check_vma=False,
    )
```

profile of v0, /device:TPU:10, one launch (start us, length us, event | category | flops | bytes accessed | tf_op | source)
XLA Modules:
  0.0 719.9 jit_solution(8978130539700495041)
XLA Ops:
  2.7 3.6 collective-permute-start
  7.7 11.4 %collective-permute-start.2 = (f32[18,1,128]{2,1,0:T(1,128)S(1)}, f32[18,1,128]{2,1,0:T(1,128)S(1)}, u32[]{:S(2)}, u32[]{:S(2)}) collective-permute-start(f32[18,1,128]{2,1,0:T(1,128)S(1)} %get-tuple-element.64), channel_id=1, source_target_pairs={{1,0},{2,1},{3,2},{4,3},{5,4},{6,5},{7,6},{8,7},{9,8},{10,9},{11,1... | collective-permute-start | bytes 27656 | tf_op jit(solution)/shard_map/ppermute | solution.py:21
  21.2 18.8 %reshape.93 = f32[8,2,16,2,64,2]{5,4,3,2,1,0:T(8,128)} reshape(f32[16,32,128]{2,1,0:T(8,128)} %param.3) | data formatting | bytes 524288 | tf_op jit(solution)/shard_map/reshape | solution.py:61
  40.0 7.0 reduce_sum.231
  47.7 3.3 collective-permute-start.4
  56.8 5.7 collective-permute-start.6
  76.0 3.2 collective-permute-start.8
  81.9 6.0 collective-permute-start.14
  89.9 6.0 collective-permute-start.10
  98.7 4.8 collective-permute-done.11
  105.4 18.1 %reshape.92 = f32[8,2,16,2,64,2]{5,4,3,2,1,0:T(8,128)} reshape(f32[16,32,128]{2,1,0:T(8,128)S(1)} %fusion.22) | data formatting | bytes 524288 | tf_op jit(solution)/shard_map/reshape | solution.py:61
  123.5 7.0 reduce_sum.230
  140.2 3.9 collective-permute-start.19
  155.6 4.0 collective-permute-start.26
  161.6 6.0 collective-permute-start.22
  170.5 4.7 collective-permute-done.23
  190.5 3.9 collective-permute-start.31
  204.8 4.0 collective-permute-start.38
  210.8 6.0 collective-permute-start.34
  218.9 5.6 collective-permute-done.35
  235.2 3.9 collective-permute-start.43
  239.1 79.6 %all_gather.7 = f32[2,256,16]{2,0,1:T(2,128)S(1)} all-gather(f32[2,4,16]{2,0,1:T(2,128)S(1)} %copy.324), channel_id=1, replica_groups=mesh['gx'=8,'yz'=64] {'yz'}, dimensions={1}, use_global_device_ids=true | all-gather | bytes 33280 | tf_op jit(solution)/shard_map/all_gather | solution.py:133
  325.7 4.6 collective-permute-start.46
  338.1 80.3 %all_gather.6 = f32[2,256,16]{2,0,1:T(2,128)S(1)} all-gather(f32[2,4,16]{2,0,1:T(2,128)S(1)} %copy.321), channel_id=1, replica_groups=mesh['gx'=8,'yz'=64] {'yz'}, dimensions={1}, use_global_device_ids=true | all-gather | bytes 33280 | tf_op jit(solution)/shard_map/all_gather | solution.py:132
  428.3 11.3 %all-reduce.29 = (f32[]{:T(128)}, f32[]{:T(128)}) all-reduce(f32[]{:T(128)} %get-tuple-element.115, f32[]{:T(128)} %get-tuple-element.36), channel_id=1, replica_groups=mesh['gx'=8,'yz'=64] {'gx'}, use_global_device_ids=true, to_apply=%region_9.10 | all-reduce | flops 2 | bytes 16 | tf_op jit(solution)/shard_map/psum | solution.py:89
  440.9 3.8 collective-permute-start.52
  450.4 11.0 %all-reduce.28 = (f32[]{:T(128)}, f32[]{:T(128)}) all-reduce(f32[]{:T(128)} %get-tuple-element.12, f32[]{:T(128)} %get-tuple-element.11), channel_id=1, replica_groups=mesh['gx'=8,'yz'=64] {'gx'}, use_global_device_ids=true, to_apply=%region_15.16 | all-reduce | flops 2 | bytes 16 | tf_op jit(solution)/shard_map/psum | solution.py:103
  465.8 11.9 %psum.116 = f32[]{:T(128)} all-reduce(f32[]{:T(128)} %multiply_reduce_fusion.11), channel_id=1, replica_groups=mesh['gx'=8,'yz'=64] {'gx'}, use_global_device_ids=true, to_apply=%region_19.20 | all-reduce | flops 1 | bytes 8 | tf_op jit(solution)/shard_map/psum | solution.py:109
  479.1 4.7 collective-permute-start.54
  489.4 10.7 %psum.117 = f32[]{:T(128)} all-reduce(f32[]{:T(128)} %get-tuple-element.33), channel_id=1, replica_groups=mesh['gx'=8,'yz'=64] {'gx'}, use_global_device_ids=true, to_apply=%region_21.22 | all-reduce | flops 1 | bytes 8 | tf_op jit(solution)/shard_map/psum | solution.py:100
  509.7 11.0 %all-reduce.27 = (f32[]{:T(128)}, f32[]{:T(128)}) all-reduce(f32[]{:T(128)} %get-tuple-element.10, f32[]{:T(128)} %get-tuple-element.9), channel_id=1, replica_groups=mesh['gx'=8,'yz'=64] {'gx'}, use_global_device_ids=true, to_apply=%region_23.24 | all-reduce | flops 2 | bytes 16 | tf_op jit(solution)/shard_map/psum | solution.py:103
  525.1 12.1 %psum.120 = f32[]{:T(128)} all-reduce(f32[]{:T(128)} %get-tuple-element.30), channel_id=1, replica_groups=mesh['gx'=8,'yz'=64] {'gx'}, use_global_device_ids=true, to_apply=%region_27.28 | all-reduce | flops 1 | bytes 8 | tf_op jit(solution)/shard_map/psum | solution.py:109
  538.4 4.7 collective-permute-start.58
  548.9 10.7 %psum.121 = f32[]{:T(128)} all-reduce(f32[]{:T(128)} %get-tuple-element.28), channel_id=1, replica_groups=mesh['gx'=8,'yz'=64] {'gx'}, use_global_device_ids=true, to_apply=%region_29.30 | all-reduce | flops 1 | bytes 8 | tf_op jit(solution)/shard_map/psum | solution.py:100
  569.3 11.0 %all-reduce.26 = (f32[]{:T(128)}, f32[]{:T(128)}) all-reduce(f32[]{:T(128)} %get-tuple-element.8, f32[]{:T(128)} %get-tuple-element.7), channel_id=1, replica_groups=mesh['gx'=8,'yz'=64] {'gx'}, use_global_device_ids=true, to_apply=%region_31.32 | all-reduce | flops 2 | bytes 16 | tf_op jit(solution)/shard_map/psum | solution.py:103
  584.7 12.1 %psum.124 = f32[]{:T(128)} all-reduce(f32[]{:T(128)} %get-tuple-element.25), channel_id=1, replica_groups=mesh['gx'=8,'yz'=64] {'gx'}, use_global_device_ids=true, to_apply=%region_35.36 | all-reduce | flops 1 | bytes 8 | tf_op jit(solution)/shard_map/psum | solution.py:109
  598.2 4.7 collective-permute-start.62
  608.7 10.7 %psum.125 = f32[]{:T(128)} all-reduce(f32[]{:T(128)} %get-tuple-element.23), channel_id=1, replica_groups=mesh['gx'=8,'yz'=64] {'gx'}, use_global_device_ids=true, to_apply=%region_37.38 | all-reduce | flops 1 | bytes 8 | tf_op jit(solution)/shard_map/psum | solution.py:100
  629.1 11.0 %all-reduce.25 = (f32[]{:T(128)}, f32[]{:T(128)}) all-reduce(f32[]{:T(128)} %get-tuple-element.6, f32[]{:T(128)} %get-tuple-element.5), channel_id=1, replica_groups=mesh['gx'=8,'yz'=64] {'gx'}, use_global_device_ids=true, to_apply=%region_39.40 | all-reduce | flops 2 | bytes 16 | tf_op jit(solution)/shard_map/psum | solution.py:103
  641.8 3.3 collective-permute-start.66
  650.1 4.6 collective-permute-start.68
  656.6 5.6 collective-permute-done.69
  671.4 3.9 collective-permute-start.73
  675.4 3.7 collective-permute-done.73
  689.4 3.9 collective-permute-start.77
  693.3 3.7 collective-permute-done.77
  709.9 3.9 collective-permute-start.81
  713.8 3.7 collective-permute-done.81
  (322 shorter events, 217.0 us)
Async XLA Ops:
  7.7 39.3 %collective-permute-start.2 = (f32[18,1,128]{2,1,0:T(1,128)S(1)}, f32[18,1,128]{2,1,0:T(1,128)S(1)}, u32[]{:S(2)}, u32[]{:S(2)}) collective-permute-start(f32[18,1,128]{2,1,0:T(1,128)S(1)} %get-tuple-element.64), channel_id=1, source_target_pairs={{1,0},{2,1},{3,2},{4,3},{5,4},{6,5},{7,6},{8,7},{9,8},{10,9},{11,1... | collective-permute-start | bytes 27656 | tf_op jit(solution)/shard_map/ppermute | solution.py:21
  19.2 27.9 %collective-permute-start.3 = (f32[18,1,128]{2,1,0:T(1,128)S(1)}, f32[18,1,128]{2,1,0:T(1,128)S(1)}, u32[]{:S(2)}, u32[]{:S(2)}) collective-permute-start(f32[18,1,128]{2,1,0:T(1,128)S(1)} %get-tuple-element.63), channel_id=1, source_target_pairs={{0,1},{1,2},{2,3},{3,4},{4,5},{5,6},{6,7},{7,8},{8,9},{9,10},{10,1... | collective-permute-start | bytes 27656 | tf_op jit(solution)/shard_map/ppermute | solution.py:19
  56.8 15.6 %collective-permute-start.6 = (f32[18,1,128]{2,1,0:T(1,128)}, f32[18,1,128]{2,1,0:T(1,128)}, u32[]{:S(2)}, u32[]{:S(2)}) collective-permute-start(f32[18,1,128]{2,1,0:T(1,128)} %get-tuple-element.62), channel_id=1, source_target_pairs={{1,0},{2,1},{3,2},{4,3},{5,4},{6,5},{7,6},{8,7},{9,8},{10,9},{11,1... | collective-permute-start | bytes 27656 | tf_op jit(solution)/shard_map/ppermute | solution.py:21
  62.6 9.9 %collective-permute-start.7 = (f32[18,1,128]{2,1,0:T(1,128)}, f32[18,1,128]{2,1,0:T(1,128)}, u32[]{:S(2)}, u32[]{:S(2)}) collective-permute-start(f32[18,1,128]{2,1,0:T(1,128)} %get-tuple-element.61), channel_id=1, source_target_pairs={{0,1},{1,2},{2,3},{3,4},{4,5},{5,6},{6,7},{7,8},{8,9},{9,10},{10,1... | collective-permute-start | bytes 27656 | tf_op jit(solution)/shard_map/ppermute | solution.py:19
  65.1 16.0 %collective-permute-start.12 = (f32[1,16,64]{2,1,0:T(8,128)}, f32[1,16,64]{2,1,0:T(8,128)}, u32[]{:S(2)}, u32[]{:S(2)}) collective-permute-start(f32[1,16,64]{2,1,0:T(8,128)} %get-tuple-element.88), channel_id=1, source_target_pairs={{64,0},{128,64},{192,128},{256,192},{320,256},{384,320},{448,384},... | collective-permute-start | bytes 12296 | tf_op jit(solution)/shard_map/ppermute | solution.py:21
  67.0 14.1 %collective-permute-start.13 = (f32[1,16,64]{2,1,0:T(8,128)}, f32[1,16,64]{2,1,0:T(8,128)}, u32[]{:S(2)}, u32[]{:S(2)}) collective-permute-start(f32[1,16,64]{2,1,0:T(8,128)} %get-tuple-element.87), channel_id=1, source_target_pairs={{0,64},{64,128},{128,192},{192,256},{256,320},{320,384},{384,448},... | collective-permute-start | bytes 12296 | tf_op jit(solution)/shard_map/ppermute | solution.py:19
  76.0 13.8 %collective-permute-start.8 = (f32[1,32,128]{2,1,0:T(8,128)S(1)}, f32[1,32,128]{2,1,0:T(8,128)S(1)}, u32[]{:S(2)}, u32[]{:S(2)}) collective-permute-start(f32[1,32,128]{2,1,0:T(8,128)S(1)} %get-tuple-element.68), channel_id=1, source_target_pairs={{64,0},{128,64},{192,128},{256,192},{320,256},{384,320},{448,384},... | collective-permute-start | bytes 49160 | tf_op jit(solution)/shard_map/ppermute | solution.py:21
  79.2 10.6 %collective-permute-start.9 = (f32[1,32,128]{2,1,0:T(8,128)S(1)}, f32[1,32,128]{2,1,0:T(8,128)S(1)}, u32[]{:S(2)}, u32[]{:S(2)}) collective-permute-start(f32[1,32,128]{2,1,0:T(8,128)S(1)} %get-tuple-element.67), channel_id=1, source_target_pairs={{0,64},{64,128},{128,192},{192,256},{256,320},{320,384},{384,448},... | collective-permute-start | bytes 49160 | tf_op jit(solution)/shard_map/ppermute | solution.py:19
  81.9 16.0 %collective-permute-start.14 = (f32[10,1,64]{2,1,0:T(1,128)S(1)}, f32[10,1,64]{2,1,0:T(1,128)S(1)}, u32[]{:S(2)}, u32[]{:S(2)}) collective-permute-start(f32[10,1,64]{2,1,0:T(1,128)S(1)} %get-tuple-element.80), channel_id=1, source_target_pairs={{1,0},{2,1},{3,2},{4,3},{5,4},{6,5},{7,6},{8,7},{9,8},{10,9},{11,1... | collective-permute-start | bytes 7688 | tf_op jit(solution)/shard_map/ppermute | solution.py:21
  87.9 10.0 %collective-permute-start.15 = (f32[10,1,64]{2,1,0:T(1,128)S(1)}, f32[10,1,64]{2,1,0:T(1,128)S(1)}, u32[]{:S(2)}, u32[]{:S(2)}) collective-permute-start(f32[10,1,64]{2,1,0:T(1,128)S(1)} %get-tuple-element.79), channel_id=1, source_target_pairs={{0,1},{1,2},{2,3},{3,4},{4,5},{5,6},{6,7},{7,8},{8,9},{9,10},{10,1... | collective-permute-start | bytes 7688 | tf_op jit(solution)/shard_map/ppermute | solution.py:19
  89.9 8.9 %collective-permute-start.10 = (f32[18,1,128]{2,1,0:T(1,128)S(1)}, f32[18,1,128]{2,1,0:T(1,128)S(1)}, u32[]{:S(2)}, u32[]{:S(2)}) collective-permute-start(f32[18,1,128]{2,1,0:T(1,128)S(1)} %get-tuple-element.60), channel_id=1, source_target_pairs={{1,0},{2,1},{3,2},{4,3},{5,4},{6,5},{7,6},{8,7},{9,8},{10,9},{11,1... | collective-permute-start | bytes 27656 | tf_op jit(solution)/shard_map/ppermute | solution.py:21
  95.9 7.7 %collective-permute-start.11 = (f32[18,1,128]{2,1,0:T(1,128)S(1)}, f32[18,1,128]{2,1,0:T(1,128)S(1)}, u32[]{:S(2)}, u32[]{:S(2)}) collective-permute-start(f32[18,1,128]{2,1,0:T(1,128)S(1)} %get-tuple-element.59), channel_id=1, source_target_pairs={{0,1},{1,2},{2,3},{3,4},{4,5},{5,6},{6,7},{7,8},{8,9},{9,10},{10,1... | collective-permute-start | bytes 27656 | tf_op jit(solution)/shard_map/ppermute | solution.py:19
  138.3 11.1 %collective-permute-start.18 = (f32[10,1,64]{2,1,0:T(1,128)S(1)}, f32[10,1,64]{2,1,0:T(1,128)S(1)}, u32[]{:S(2)}, u32[]{:S(2)}) collective-permute-start(f32[10,1,64]{2,1,0:T(1,128)S(1)} %get-tuple-element.78), channel_id=1, source_target_pairs={{1,0},{2,1},{3,2},{4,3},{5,4},{6,5},{7,6},{8,7},{9,8},{10,9},{11,1... | collective-permute-start | bytes 7688 | tf_op jit(solution)/shard_map/ppermute | solution.py:21
  140.2 9.2 %collective-permute-start.19 = (f32[10,1,64]{2,1,0:T(1,128)S(1)}, f32[10,1,64]{2,1,0:T(1,128)S(1)}, u32[]{:S(2)}, u32[]{:S(2)}) collective-permute-start(f32[10,1,64]{2,1,0:T(1,128)S(1)} %get-tuple-element.77), channel_id=1, source_target_pairs={{0,1},{1,2},{2,3},{3,4},{4,5},{5,6},{6,7},{7,8},{8,9},{9,10},{10,1... | collective-permute-start | bytes 7688 | tf_op jit(solution)/shard_map/ppermute | solution.py:19
  144.2 11.3 %collective-permute-start.24 = (f32[1,8,32]{2,1,0:T(8,128)S(1)}, f32[1,8,32]{2,1,0:T(8,128)S(1)}, u32[]{:S(2)}, u32[]{:S(2)}) collective-permute-start(f32[1,8,32]{2,1,0:T(8,128)S(1)} %get-tuple-element.104), channel_id=1, source_target_pairs={{64,0},{128,64},{192,128},{256,192},{320,256},{384,320},{448,384},... | collective-permute-start | bytes 3080 | tf_op jit(solution)/shard_map/ppermute | solution.py:21
  146.1 9.4 %collective-permute-start.25 = (f32[1,8,32]{2,1,0:T(8,128)S(1)}, f32[1,8,32]{2,1,0:T(8,128)S(1)}, u32[]{:S(2)}, u32[]{:S(2)}) collective-permute-start(f32[1,8,32]{2,1,0:T(8,128)S(1)} %get-tuple-element.103), channel_id=1, source_target_pairs={{0,64},{64,128},{128,192},{192,256},{256,320},{320,384},{384,448},... | collective-permute-start | bytes 3080 | tf_op jit(solution)/shard_map/ppermute | solution.py:19
  150.4 11.1 %collective-permute-start.20 = (f32[1,16,64]{2,1,0:T(8,128)S(1)}, f32[1,16,64]{2,1,0:T(8,128)S(1)}, u32[]{:S(2)}, u32[]{:S(2)}) collective-permute-start(f32[1,16,64]{2,1,0:T(8,128)S(1)} %get-tuple-element.84), channel_id=1, source_target_pairs={{64,0},{128,64},{192,128},{256,192},{320,256},{384,320},{448,384},... | collective-permute-start | bytes 12296 | tf_op jit(solution)/shard_map/ppermute | solution.py:21
  153.6 8.0 %collective-permute-start.21 = (f32[1,16,64]{2,1,0:T(8,128)S(1)}, f32[1,16,64]{2,1,0:T(8,128)S(1)}, u32[]{:S(2)}, u32[]{:S(2)}) collective-permute-start(f32[1,16,64]{2,1,0:T(8,128)S(1)} %get-tuple-element.83), channel_id=1, source_target_pairs={{0,64},{64,128},{128,192},{192,256},{256,320},{320,384},{384,448},... | collective-permute-start | bytes 12296 | tf_op jit(solution)/shard_map/ppermute | solution.py:19
  155.6 14.2 %collective-permute-start.26 = (f32[6,1,32]{2,1,0:T(1,128)S(1)}, f32[6,1,32]{2,1,0:T(1,128)S(1)}, u32[]{:S(2)}, u32[]{:S(2)}) collective-permute-start(f32[6,1,32]{2,1,0:T(1,128)S(1)} %get-tuple-element.96), channel_id=1, source_target_pairs={{1,0},{2,1},{3,2},{4,3},{5,4},{6,5},{7,6},{8,7},{9,8},{10,9},{11,1... | collective-permute-start | bytes 2312 | tf_op jit(solution)/shard_map/ppermute | solution.py:21
  159.6 10.1 %collective-permute-start.27 = (f32[6,1,32]{2,1,0:T(1,128)S(1)}, f32[6,1,32]{2,1,0:T(1,128)S(1)}, u32[]{:S(2)}, u32[]{:S(2)}) collective-permute-start(f32[6,1,32]{2,1,0:T(1,128)S(1)} %get-tuple-element.95), channel_id=1, source_target_pairs={{0,1},{1,2},{2,3},{3,4},{4,5},{5,6},{6,7},{7,8},{8,9},{9,10},{10,1... | collective-permute-start | bytes 2312 | tf_op jit(solution)/shard_map/ppermute | solution.py:19
  161.6 8.9 %collective-permute-start.22 = (f32[10,1,64]{2,1,0:T(1,128)S(1)}, f32[10,1,64]{2,1,0:T(1,128)S(1)}, u32[]{:S(2)}, u32[]{:S(2)}) collective-permute-start(f32[10,1,64]{2,1,0:T(1,128)S(1)} %get-tuple-element.76), channel_id=1, source_target_pairs={{1,0},{2,1},{3,2},{4,3},{5,4},{6,5},{7,6},{8,7},{9,8},{10,9},{11,1... | collective-permute-start | bytes 7688 | tf_op jit(solution)/shard_map/ppermute | solution.py:21
  167.6 7.6 %collective-permute-start.23 = (f32[10,1,64]{2,1,0:T(1,128)S(1)}, f32[10,1,64]{2,1,0:T(1,128)S(1)}, u32[]{:S(2)}, u32[]{:S(2)}) collective-permute-start(f32[10,1,64]{2,1,0:T(1,128)S(1)} %get-tuple-element.75), channel_id=1, source_target_pairs={{0,1},{1,2},{2,3},{3,4},{4,5},{5,6},{6,7},{7,8},{8,9},{9,10},{10,1... | collective-permute-start | bytes 7688 | tf_op jit(solution)/shard_map/ppermute | solution.py:19
  188.6 10.2 %collective-permute-start.30 = (f32[6,1,32]{2,1,0:T(1,128)S(1)}, f32[6,1,32]{2,1,0:T(1,128)S(1)}, u32[]{:S(2)}, u32[]{:S(2)}) collective-permute-start(f32[6,1,32]{2,1,0:T(1,128)S(1)} %get-tuple-element.94), channel_id=1, source_target_pairs={{1,0},{2,1},{3,2},{4,3},{5,4},{6,5},{7,6},{8,7},{9,8},{10,9},{11,1... | collective-permute-start | bytes 2312 | tf_op jit(solution)/shard_map/ppermute | solution.py:21
  190.5 8.3 %collective-permute-start.31 = (f32[6,1,32]{2,1,0:T(1,128)S(1)}, f32[6,1,32]{2,1,0:T(1,128)S(1)}, u32[]{:S(2)}, u32[]{:S(2)}) collective-permute-start(f32[6,1,32]{2,1,0:T(1,128)S(1)} %get-tuple-element.93), channel_id=1, source_target_pairs={{0,1},{1,2},{2,3},{3,4},{4,5},{5,6},{6,7},{7,8},{8,9},{9,10},{10,1... | collective-permute-start | bytes 2312 | tf_op jit(solution)/shard_map/ppermute | solution.py:19
  194.4 10.4 %collective-permute-start.36 = (f32[1,4,16]{2,1,0:T(4,128)S(1)}, f32[1,4,16]{2,1,0:T(4,128)S(1)}, u32[]{:S(2)}, u32[]{:S(2)}) collective-permute-start(f32[1,4,16]{2,1,0:T(4,128)S(1)} %get-tuple-element.122), channel_id=1, source_target_pairs={{64,0},{128,64},{192,128},{256,192},{320,256},{384,320},{448,384},... | collective-permute-start | bytes 776 | tf_op jit(solution)/shard_map/ppermute | solution.py:21
  196.3 8.5 %collective-permute-start.37 = (f32[1,4,16]{2,1,0:T(4,128)S(1)}, f32[1,4,16]{2,1,0:T(4,128)S(1)}, u32[]{:S(2)}, u32[]{:S(2)}) collective-permute-start(f32[1,4,16]{2,1,0:T(4,128)S(1)} %get-tuple-element.121), channel_id=1, source_target_pairs={{0,64},{64,128},{128,192},{192,256},{256,320},{320,384},{384,448},... | collective-permute-start | bytes 776 | tf_op jit(solution)/shard_map/ppermute | solution.py:19
  199.7 11.1 %collective-permute-start.32 = (f32[1,8,32]{2,1,0:T(8,128)S(1)}, f32[1,8,32]{2,1,0:T(8,128)S(1)}, u32[]{:S(2)}, u32[]{:S(2)}) collective-permute-start(f32[1,8,32]{2,1,0:T(8,128)S(1)} %get-tuple-element.100), channel_id=1, source_target_pairs={{64,0},{128,64},{192,128},{256,192},{320,256},{384,320},{448,384},... | collective-permute-start | bytes 3080 | tf_op jit(solution)/shard_map/ppermute | solution.py:21
  202.9 7.9 %collective-permute-start.33 = (f32[1,8,32]{2,1,0:T(8,128)S(1)}, f32[1,8,32]{2,1,0:T(8,128)S(1)}, u32[]{:S(2)}, u32[]{:S(2)}) collective-permute-start(f32[1,8,32]{2,1,0:T(8,128)S(1)} %get-tuple-element.99), channel_id=1, source_target_pairs={{0,64},{64,128},{128,192},{192,256},{256,320},{320,384},{384,448},... | collective-permute-start | bytes 3080 | tf_op jit(solution)/shard_map/ppermute | solution.py:19
  204.8 14.0 %collective-permute-start.38 = (f32[4,1,16]{2,1,0:T(1,128)S(1)}, f32[4,1,16]{2,1,0:T(1,128)S(1)}, u32[]{:S(2)}, u32[]{:S(2)}) collective-permute-start(f32[4,1,16]{2,1,0:T(1,128)S(1)} %get-tuple-element.112), channel_id=1, source_target_pairs={{1,0},{2,1},{3,2},{4,3},{5,4},{6,5},{7,6},{8,7},{9,8},{10,9},{11,1... | collective-permute-start | bytes 776 | tf_op jit(solution)/shard_map/ppermute | solution.py:21
  208.9 9.9 %collective-permute-start.39 = (f32[4,1,16]{2,1,0:T(1,128)S(1)}, f32[4,1,16]{2,1,0:T(1,128)S(1)}, u32[]{:S(2)}, u32[]{:S(2)}) collective-permute-start(f32[4,1,16]{2,1,0:T(1,128)S(1)} %get-tuple-element.111), channel_id=1, source_target_pairs={{0,1},{1,2},{2,3},{3,4},{4,5},{5,6},{6,7},{7,8},{8,9},{9,10},{10,1... | collective-permute-start | bytes 776 | tf_op jit(solution)/shard_map/ppermute | solution.py:19
  210.8 8.1 %collective-permute-start.34 = (f32[6,1,32]{2,1,0:T(1,128)S(1)}, f32[6,1,32]{2,1,0:T(1,128)S(1)}, u32[]{:S(2)}, u32[]{:S(2)}) collective-permute-start(f32[6,1,32]{2,1,0:T(1,128)S(1)} %get-tuple-element.92), channel_id=1, source_target_pairs={{1,0},{2,1},{3,2},{4,3},{5,4},{6,5},{7,6},{8,7},{9,8},{10,9},{11,1... | collective-permute-start | bytes 2312 | tf_op jit(solution)/shard_map/ppermute | solution.py:21
  216.9 7.6 %collective-permute-start.35 = (f32[6,1,32]{2,1,0:T(1,128)S(1)}, f32[6,1,32]{2,1,0:T(1,128)S(1)}, u32[]{:S(2)}, u32[]{:S(2)}) collective-permute-start(f32[6,1,32]{2,1,0:T(1,128)S(1)} %get-tuple-element.91), channel_id=1, source_target_pairs={{0,1},{1,2},{2,3},{3,4},{4,5},{5,6},{6,7},{7,8},{8,9},{9,10},{10,1... | collective-permute-start | bytes 2312 | tf_op jit(solution)/shard_map/ppermute | solution.py:19
  233.3 85.4 %collective-permute-start.42 = (f32[4,1,16]{2,1,0:T(1,128)S(1)}, f32[4,1,16]{2,1,0:T(1,128)S(1)}, u32[]{:S(2)}, u32[]{:S(2)}) collective-permute-start(f32[4,1,16]{2,1,0:T(1,128)S(1)} %get-tuple-element.110), channel_id=1, source_target_pairs={{1,0},{2,1},{3,2},{4,3},{5,4},{6,5},{7,6},{8,7},{9,8},{10,9},{11,1... | collective-permute-start | bytes 776 | tf_op jit(solution)/shard_map/ppermute | solution.py:21
  235.2 83.5 %collective-permute-start.43 = (f32[4,1,16]{2,1,0:T(1,128)S(1)}, f32[4,1,16]{2,1,0:T(1,128)S(1)}, u32[]{:S(2)}, u32[]{:S(2)}) collective-permute-start(f32[4,1,16]{2,1,0:T(1,128)S(1)} %get-tuple-element.109), channel_id=1, source_target_pairs={{0,1},{1,2},{2,3},{3,4},{4,5},{5,6},{6,7},{7,8},{8,9},{9,10},{10,1... | collective-permute-start | bytes 776 | tf_op jit(solution)/shard_map/ppermute | solution.py:19
  318.9 6.0 collective-permute-start.44
  325.7 10.9 %collective-permute-start.46 = (f32[4,1,16]{2,1,0:T(1,128)S(1)}, f32[4,1,16]{2,1,0:T(1,128)S(1)}, u32[]{:S(2)}, u32[]{:S(2)}) collective-permute-start(f32[4,1,16]{2,1,0:T(1,128)S(1)} %get-tuple-element.108), channel_id=1, source_target_pairs={{1,0},{2,1},{3,2},{4,3},{5,4},{6,5},{7,6},{8,7},{9,8},{10,9},{11,1... | collective-permute-start | bytes 776 | tf_op jit(solution)/shard_map/ppermute | solution.py:21
  330.3 7.6 %collective-permute-start.47 = (f32[4,1,16]{2,1,0:T(1,128)S(1)}, f32[4,1,16]{2,1,0:T(1,128)S(1)}, u32[]{:S(2)}, u32[]{:S(2)}) collective-permute-start(f32[4,1,16]{2,1,0:T(1,128)S(1)} %get-tuple-element.107), channel_id=1, source_target_pairs={{0,1},{1,2},{2,3},{3,4},{4,5},{5,6},{6,7},{7,8},{8,9},{9,10},{10,1... | collective-permute-start | bytes 776 | tf_op jit(solution)/shard_map/ppermute | solution.py:19
  332.3 92.7 %collective-permute-start.48 = (f32[1,128,8]{1,2,0:T(8,128)S(1)}, f32[1,128,8]{1,2,0:T(8,128)S(1)}, u32[]{:S(2)}, u32[]{:S(2)}) collective-permute-start(f32[1,128,8]{1,2,0:T(8,128)S(1)} %multiply_bitcast_fusion), channel_id=1, source_target_pairs={{64,0},{128,64},{192,128},{256,192},{320,256},{384,320},{448,384},... | collective-permute-start | bytes 12296 | tf_op jit(solution)/shard_map/ppermute | solution.py:21
  334.3 90.7 %collective-permute-start.50 = (f32[1,128,8]{1,2,0:T(8,128)S(1)}, f32[1,128,8]{1,2,0:T(8,128)S(1)}, u32[]{:S(2)}, u32[]{:S(2)}) collective-permute-start(f32[1,128,8]{1,2,0:T(8,128)S(1)} %multiply_bitcast_fusion), channel_id=1, source_target_pairs={{0,64},{64,128},{128,192},{192,256},{256,320},{320,384},{384,448},... | collective-permute-start | bytes 12296 | tf_op jit(solution)/shard_map/ppermute | solution.py:19
  479.1 6.6 collective-permute-start.54
  538.4 6.6 collective-permute-start.58
  598.2 6.6 collective-permute-start.62
  650.1 6.5 collective-permute-start.68
  654.7 7.6 %collective-permute-start.69 = (f32[4,1,16]{2,1,0:T(1,128)S(1)}, f32[4,1,16]{2,1,0:T(1,128)S(1)}, u32[]{:S(2)}, u32[]{:S(2)}) collective-permute-start(f32[4,1,16]{2,1,0:T(1,128)S(1)} %get-tuple-element.105), channel_id=1, source_target_pairs={{0,1},{1,2},{2,3},{3,4},{4,5},{5,6},{6,7},{7,8},{8,9},{9,10},{10,1... | collective-permute-start | bytes 776 | tf_op jit(solution)/shard_map/ppermute | solution.py:19
  669.5 5.9 collective-permute-start.72
  671.4 7.6 %collective-permute-start.73 = (f32[6,1,32]{2,1,0:T(1,128)S(1)}, f32[6,1,32]{2,1,0:T(1,128)S(1)}, u32[]{:S(2)}, u32[]{:S(2)}) collective-permute-start(f32[6,1,32]{2,1,0:T(1,128)S(1)} %get-tuple-element.89), channel_id=1, source_target_pairs={{0,1},{1,2},{2,3},{3,4},{4,5},{5,6},{6,7},{7,8},{8,9},{9,10},{10,1... | collective-permute-start | bytes 2312 | tf_op jit(solution)/shard_map/ppermute | solution.py:19
  689.4 7.6 %collective-permute-start.77 = (f32[10,1,64]{2,1,0:T(1,128)S(1)}, f32[10,1,64]{2,1,0:T(1,128)S(1)}, u32[]{:S(2)}, u32[]{:S(2)}) collective-permute-start(f32[10,1,64]{2,1,0:T(1,128)S(1)} %get-tuple-element.73), channel_id=1, source_target_pairs={{0,1},{1,2},{2,3},{3,4},{4,5},{5,6},{6,7},{7,8},{8,9},{9,10},{10,1... | collective-permute-start | bytes 7688 | tf_op jit(solution)/shard_map/ppermute | solution.py:19
  709.9 7.7 %collective-permute-start.81 = (f32[18,1,128]{2,1,0:T(1,128)S(1)}, f32[18,1,128]{2,1,0:T(1,128)S(1)}, u32[]{:S(2)}, u32[]{:S(2)}) collective-permute-start(f32[18,1,128]{2,1,0:T(1,128)S(1)} %get-tuple-element.57), channel_id=1, source_target_pairs={{0,1},{1,2},{2,3},{3,4},{4,5},{5,6},{6,7},{7,8},{8,9},{9,10},{10,1... | collective-permute-start | bytes 27656 | tf_op jit(solution)/shard_map/ppermute | solution.py:19
  (55 other events, 1854.1 us)
where the time goes:
time: 724 us; the launch traced here: 720 us
  blocking collectives  283 us (39%)
  starting transfers between devices  236 us (33%)
  waiting for transfers between devices  78.5 us (11%)
  local copies, waits for them, and re-layouts  50.6 us (7%)
  other arithmetic  48.4 us (7%)
  between operations  23.8 us (3%)
    ppermute x41, starting transfers between devices, padded_2(): lax.ppermute(head, axis, [((i + 1) % count, i) for i in range(ends)])  139 us
    ppermute x41, starting transfers between devices, padded_2(): lax.ppermute(tail, axis, [(i, (i + 1) % count) for i in range(ends)])  96.7 us
    all_gather x1, blocking collectives, per_device(): lax.all_gather(residual, 'yz', axis=1, tiled=True)  80.3 us
    all_gather x1, blocking collectives, per_device(): lax.all_gather(weight, 'yz', axis=1, tiled=True)  79.6 us
    ppermute x41, waiting for transfers between devices, padded_2(): lax.ppermute(tail, axis, [(i, (i + 1) % count) for i in range(ends)])  78 us
    psum x4, blocking collectives, stabilized_solve(): rho_now = lax.psum(jnp.sum(source * residual), 'gx')  47.4 us
    psum x4, blocking collectives, stabilized_solve(): lax.psum((jnp.sum(bent_image * middle), jnp.sum(bent_image * bent_image))...  43.9 us
    reshape x4, local copies, waits for them, and re-layouts, restrict(): values.reshape(values.shape[0] // 2, 2, values.shape[1] // 2, 2, values.s...  40 us
  transfers between devices with their start and end apart: 82, of which 26 were waited for; matrix products, arithmetic and copies ran while one was open for 6% of the time, Pallas kernels for 0%

commit v1 on v0

--- a/solution.py
+++ b/solution.py
@@ -129,7 +129,9 @@
         stored.append((source, iterate, face_list, diagonal, merged))
         if level_index == LEVELS - 1:
             residual, weight = (
-                lax.all_gather(residual, "yz", axis=1, tiled=True),
+                jnp.concatenate(
+                    lax.all_to_all(jnp.stack([residual] * lax.axis_size("yz")), "yz", 0, 0), axis=1
+                ),
                 lax.all_gather(weight, "yz", axis=1, tiled=True),
             )
         source = restrict(residual)

time: 724 us -> 665 us (0.919)
  blocking collectives: 283 us -> 203 us
  waiting for transfers between devices: 78.5 us -> 92.4 us
    all_gather x1 -> x0, blocking collectives: 80.3 us -> none  [per_device(): lax.all_gather(residual, 'yz', axis=1, tiled=True)]
    all_to_all x0 -> x1, waiting for transfers between devices: none -> 9.02 us  [per_device(): lax.all_to_all(jnp.stack([residual] * lax.axis_size('yz')), 'yz', 0, 0)]
  transfers between devices with their start and end apart: 82 -> 83, of which waited for: 26 -> 27; matrix products, arithmetic and copies ran while one was open for 6% -> 7% of each run, Pallas kernels for 0% -> 0%
where the time goes in v1:
time: 665 us; the launch traced here: 661 us
  starting transfers between devices  240 us (36%)
  blocking collectives  203 us (31%)
  waiting for transfers between devices  92.4 us (14%)
  local copies, waits for them, and re-layouts  51.5 us (8%)
  other arithmetic  50.8 us (8%)
  between operations  23.3 us (4%)
    ppermute x41, starting transfers between devices, padded_2(): lax.ppermute(head, axis, [((i + 1) % count, i) for i in range(ends)])  137 us
    ppermute x41, starting transfers between devices, padded_2(): lax.ppermute(tail, axis, [(i, (i + 1) % count) for i in range(ends)])  97.5 us
    ppermute x41, waiting for transfers between devices, padded_2(): lax.ppermute(tail, axis, [(i, (i + 1) % count) for i in range(ends)])  82.8 us
    all_gather x1, blocking collectives, per_device(): lax.all_gather(weight, 'yz', axis=1, tiled=True)  79.5 us
    psum x4, blocking collectives, stabilized_solve(): rho_now = lax.psum(jnp.sum(source * residual), 'gx')  47.4 us
    psum x4, blocking collectives, stabilized_solve(): lax.psum((jnp.sum(bent_image * middle), jnp.sum(bent_image * bent_image))...  43.8 us
    reshape x4, local copies, waits for them, and re-layouts, restrict(): values.reshape(values.shape[0] // 2, 2, values.shape[1] // 2, 2, values.s...  40.1 us
    psum x3, blocking collectives, stabilized_solve(): step_alpha = rho_now / lax.psum(jnp.sum(source * applied), 'gx')  31.9 us
  transfers between devices with their start and end apart: 83, of which 27 were waited for; matrix products, arithmetic and copies ran while one was open for 7% of the time, Pallas kernels for 0%

profile of v1, /device:TPU:10, one launch (start us, length us, event | category | flops | bytes accessed | tf_op | source)
XLA Modules:
  0.0 660.9 jit_solution(18156226198747145318)
XLA Ops:
  2.7 3.6 collective-permute-start
  7.7 11.4 %collective-permute-start.2 = (f32[18,1,128]{2,1,0:T(1,128)S(1)}, f32[18,1,128]{2,1,0:T(1,128)S(1)}, u32[]{:S(2)}, u32[]{:S(2)}) collective-permute-start(f32[18,1,128]{2,1,0:T(1,128)S(1)} %get-tuple-element.64), channel_id=1, source_target_pairs={{1,0},{2,1},{3,2},{4,3},{5,4},{6,5},{7,6},{8,7},{9,8},{10,9},{11,1... | collective-permute-start | bytes 27656 | tf_op jit(solution)/shard_map/ppermute | solution.py:21
  21.2 18.8 %reshape.95 = f32[8,2,16,2,64,2]{5,4,3,2,1,0:T(8,128)} reshape(f32[16,32,128]{2,1,0:T(8,128)} %param.3) | data formatting | bytes 524288 | tf_op jit(solution)/shard_map/reshape | solution.py:61
  40.1 7.0 %reduce_sum.231 = f32[8,16,64]{2,1,0:T(8,128)S(1)} reduce(f32[8,2,16,2,64,2]{5,4,3,2,1,0:T(8,128)} %reshape.95, f32[]{:T(128)} %constant.15.clone.1), dimensions={1,3,5}, to_apply=%region_1.2 | reduce | flops 57344 | bytes 294916 | tf_op jit(solution)/shard_map/reduce_sum | solution.py:63
  56.8 5.7 collective-permute-start.6
  81.8 6.0 collective-permute-start.14
  89.8 6.0 collective-permute-start.10
  98.7 4.8 collective-permute-done.11
  105.3 18.1 %reshape.94 = f32[8,2,16,2,64,2]{5,4,3,2,1,0:T(8,128)} reshape(f32[16,32,128]{2,1,0:T(8,128)S(1)} %fusion.22) | data formatting | bytes 524288 | tf_op jit(solution)/shard_map/reshape | solution.py:61
  123.4 7.0 %reduce_sum.230 = f32[8,16,64]{2,1,0:T(8,128)S(1)} reduce(f32[8,2,16,2,64,2]{5,4,3,2,1,0:T(8,128)} %reshape.94, f32[]{:T(128)} %constant.15.clone.1), dimensions={1,3,5}, to_apply=%region_0.1 | reduce | flops 57344 | bytes 294916 | tf_op jit(solution)/shard_map/reduce_sum | solution.py:63
  140.2 3.9 collective-permute-start.19
  155.5 4.0 collective-permute-start.26
  161.5 6.0 collective-permute-start.22
  170.4 4.8 collective-permute-done.23
  190.5 3.9 collective-permute-start.31
  204.9 4.0 collective-permute-start.38
  210.9 6.0 collective-permute-start.34
  218.9 5.6 collective-permute-done.35
  235.3 3.9 collective-permute-start.43
  239.2 3.6 collective-permute-done.43
  247.4 79.5 %all_gather.3 = f32[2,256,16]{2,0,1:T(2,128)S(1)} all-gather(f32[2,4,16]{2,0,1:T(2,128)S(1)} %copy.405), channel_id=1, replica_groups=mesh['gx'=8,'yz'=64] {'yz'}, dimensions={1}, use_global_device_ids=true | all-gather | bytes 33280 | tf_op jit(solution)/shard_map/all_gather | solution.py:135
  326.9 4.6 collective-permute-start.46
  335.1 4.0 collective-permute-done.47
  340.1 5.4 all-to-all-start
  349.9 9.0 %all-to-all-done = f32[64,1,128]{2,1,0:T(1,128)S(1)} async-done(((f32[64,1,128]{2,1,0:T(1,128)}), f32[64,1,128]{2,1,0:T(1,128)S(1)}, u32[]{:S(2)}, u32[]{:S(2)}) %all-to-all-start) | async-done | bytes 32800 | tf_op jit(solution)/shard_map/all_to_all | solution.py:133
  370.1 11.3 %all-reduce.29 = (f32[]{:T(128)}, f32[]{:T(128)}) all-reduce(f32[]{:T(128)} %get-tuple-element.115, f32[]{:T(128)} %get-tuple-element.36), channel_id=1, replica_groups=mesh['gx'=8,'yz'=64] {'gx'}, use_global_device_ids=true, to_apply=%region_9.10 | all-reduce | flops 2 | bytes 16 | tf_op jit(solution)/shard_map/psum | solution.py:89
  382.7 3.8 collective-permute-start.52
  392.3 10.9 %all-reduce.28 = (f32[]{:T(128)}, f32[]{:T(128)}) all-reduce(f32[]{:T(128)} %get-tuple-element.12, f32[]{:T(128)} %get-tuple-element.11), channel_id=1, replica_groups=mesh['gx'=8,'yz'=64] {'gx'}, use_global_device_ids=true, to_apply=%region_15.16 | all-reduce | flops 2 | bytes 16 | tf_op jit(solution)/shard_map/psum | solution.py:103
  407.5 11.9 %psum.116 = f32[]{:T(128)} all-reduce(f32[]{:T(128)} %multiply_reduce_fusion.11), channel_id=1, replica_groups=mesh['gx'=8,'yz'=64] {'gx'}, use_global_device_ids=true, to_apply=%region_19.20 | all-reduce | flops 1 | bytes 8 | tf_op jit(solution)/shard_map/psum | solution.py:109
  420.7 4.7 collective-permute-start.54
  431.1 10.6 %psum.117 = f32[]{:T(128)} all-reduce(f32[]{:T(128)} %get-tuple-element.33), channel_id=1, replica_groups=mesh['gx'=8,'yz'=64] {'gx'}, use_global_device_ids=true, to_apply=%region_21.22 | all-reduce | flops 1 | bytes 8 | tf_op jit(solution)/shard_map/psum | solution.py:100
  451.3 11.0 %all-reduce.27 = (f32[]{:T(128)}, f32[]{:T(128)}) all-reduce(f32[]{:T(128)} %get-tuple-element.10, f32[]{:T(128)} %get-tuple-element.9), channel_id=1, replica_groups=mesh['gx'=8,'yz'=64] {'gx'}, use_global_device_ids=true, to_apply=%region_23.24 | all-reduce | flops 2 | bytes 16 | tf_op jit(solution)/shard_map/psum | solution.py:103
  466.6 12.0 %psum.120 = f32[]{:T(128)} all-reduce(f32[]{:T(128)} %get-tuple-element.30), channel_id=1, replica_groups=mesh['gx'=8,'yz'=64] {'gx'}, use_global_device_ids=true, to_apply=%region_27.28 | all-reduce | flops 1 | bytes 8 | tf_op jit(solution)/shard_map/psum | solution.py:109
  479.8 4.7 collective-permute-start.58
  490.2 10.7 %psum.121 = f32[]{:T(128)} all-reduce(f32[]{:T(128)} %get-tuple-element.28), channel_id=1, replica_groups=mesh['gx'=8,'yz'=64] {'gx'}, use_global_device_ids=true, to_apply=%region_29.30 | all-reduce | flops 1 | bytes 8 | tf_op jit(solution)/shard_map/psum | solution.py:100
  510.6 10.9 %all-reduce.26 = (f32[]{:T(128)}, f32[]{:T(128)}) all-reduce(f32[]{:T(128)} %get-tuple-element.8, f32[]{:T(128)} %get-tuple-element.7), channel_id=1, replica_groups=mesh['gx'=8,'yz'=64] {'gx'}, use_global_device_ids=true, to_apply=%region_31.32 | all-reduce | flops 2 | bytes 16 | tf_op jit(solution)/shard_map/psum | solution.py:103
  525.9 12.1 %psum.124 = f32[]{:T(128)} all-reduce(f32[]{:T(128)} %get-tuple-element.25), channel_id=1, replica_groups=mesh['gx'=8,'yz'=64] {'gx'}, use_global_device_ids=true, to_apply=%region_35.36 | all-reduce | flops 1 | bytes 8 | tf_op jit(solution)/shard_map/psum | solution.py:109
  539.3 4.7 collective-permute-start.62
  549.7 10.6 %psum.125 = f32[]{:T(128)} all-reduce(f32[]{:T(128)} %get-tuple-element.23), channel_id=1, replica_groups=mesh['gx'=8,'yz'=64] {'gx'}, use_global_device_ids=true, to_apply=%region_37.38 | all-reduce | flops 1 | bytes 8 | tf_op jit(solution)/shard_map/psum | solution.py:100
  570.0 10.9 %all-reduce.25 = (f32[]{:T(128)}, f32[]{:T(128)}) all-reduce(f32[]{:T(128)} %get-tuple-element.6, f32[]{:T(128)} %get-tuple-element.5), channel_id=1, replica_groups=mesh['gx'=8,'yz'=64] {'gx'}, use_global_device_ids=true, to_apply=%region_39.40 | all-reduce | flops 2 | bytes 16 | tf_op jit(solution)/shard_map/psum | solution.py:103
  591.6 3.5 collective-permute-start.68
  597.5 5.2 collective-permute-done.69
  612.6 4.1 collective-permute-start.73
  616.8 3.4 collective-permute-done.73
  630.4 3.9 collective-permute-start.77
  634.3 3.7 collective-permute-done.77
  650.9 3.9 collective-permute-start.81
  654.8 3.7 collective-permute-done.81
  (353 shorter events, 228.2 us)
Async XLA Ops:
  7.7 39.3 %collective-permute-start.2 = (f32[18,1,128]{2,1,0:T(1,128)S(1)}, f32[18,1,128]{2,1,0:T(1,128)S(1)}, u32[]{:S(2)}, u32[]{:S(2)}) collective-permute-start(f32[18,1,128]{2,1,0:T(1,128)S(1)} %get-tuple-element.64), channel_id=1, source_target_pairs={{1,0},{2,1},{3,2},{4,3},{5,4},{6,5},{7,6},{8,7},{9,8},{10,9},{11,1... | collective-permute-start | bytes 27656 | tf_op jit(solution)/shard_map/ppermute | solution.py:21
  19.2 27.9 %collective-permute-start.3 = (f32[18,1,128]{2,1,0:T(1,128)S(1)}, f32[18,1,128]{2,1,0:T(1,128)S(1)}, u32[]{:S(2)}, u32[]{:S(2)}) collective-permute-start(f32[18,1,128]{2,1,0:T(1,128)S(1)} %get-tuple-element.63), channel_id=1, source_target_pairs={{0,1},{1,2},{2,3},{3,4},{4,5},{5,6},{6,7},{7,8},{8,9},{9,10},{10,1... | collective-permute-start | bytes 27656 | tf_op jit(solution)/shard_map/ppermute | solution.py:19
  56.8 15.6 %collective-permute-start.6 = (f32[18,1,128]{2,1,0:T(1,128)}, f32[18,1,128]{2,1,0:T(1,128)}, u32[]{:S(2)}, u32[]{:S(2)}) collective-permute-start(f32[18,1,128]{2,1,0:T(1,128)} %get-tuple-element.62), channel_id=1, source_target_pairs={{1,0},{2,1},{3,2},{4,3},{5,4},{6,5},{7,6},{8,7},{9,8},{10,9},{11,1... | collective-permute-start | bytes 27656 | tf_op jit(solution)/shard_map/ppermute | solution.py:21
  62.6 9.9 %collective-permute-start.7 = (f32[18,1,128]{2,1,0:T(1,128)}, f32[18,1,128]{2,1,0:T(1,128)}, u32[]{:S(2)}, u32[]{:S(2)}) collective-permute-start(f32[18,1,128]{2,1,0:T(1,128)} %get-tuple-element.61), channel_id=1, source_target_pairs={{0,1},{1,2},{2,3},{3,4},{4,5},{5,6},{6,7},{7,8},{8,9},{9,10},{10,1... | collective-permute-start | bytes 27656 | tf_op jit(solution)/shard_map/ppermute | solution.py:19
  65.1 16.0 %collective-permute-start.12 = (f32[1,16,64]{2,1,0:T(8,128)}, f32[1,16,64]{2,1,0:T(8,128)}, u32[]{:S(2)}, u32[]{:S(2)}) collective-permute-start(f32[1,16,64]{2,1,0:T(8,128)} %get-tuple-element.88), channel_id=1, source_target_pairs={{64,0},{128,64},{192,128},{256,192},{320,256},{384,320},{448,384},... | collective-permute-start | bytes 12296 | tf_op jit(solution)/shard_map/ppermute | solution.py:21
  67.0 14.0 %collective-permute-start.13 = (f32[1,16,64]{2,1,0:T(8,128)}, f32[1,16,64]{2,1,0:T(8,128)}, u32[]{:S(2)}, u32[]{:S(2)}) collective-permute-start(f32[1,16,64]{2,1,0:T(8,128)} %get-tuple-element.87), channel_id=1, source_target_pairs={{0,64},{64,128},{128,192},{192,256},{256,320},{320,384},{384,448},... | collective-permute-start | bytes 12296 | tf_op jit(solution)/shard_map/ppermute | solution.py:19
  76.0 13.8 %collective-permute-start.8 = (f32[1,32,128]{2,1,0:T(8,128)S(1)}, f32[1,32,128]{2,1,0:T(8,128)S(1)}, u32[]{:S(2)}, u32[]{:S(2)}) collective-permute-start(f32[1,32,128]{2,1,0:T(8,128)S(1)} %get-tuple-element.68), channel_id=1, source_target_pairs={{64,0},{128,64},{192,128},{256,192},{320,256},{384,320},{448,384},... | collective-permute-start | bytes 49160 | tf_op jit(solution)/shard_map/ppermute | solution.py:21
  79.1 10.7 %collective-permute-start.9 = (f32[1,32,128]{2,1,0:T(8,128)S(1)}, f32[1,32,128]{2,1,0:T(8,128)S(1)}, u32[]{:S(2)}, u32[]{:S(2)}) collective-permute-start(f32[1,32,128]{2,1,0:T(8,128)S(1)} %get-tuple-element.67), channel_id=1, source_target_pairs={{0,64},{64,128},{128,192},{192,256},{256,320},{320,384},{384,448},... | collective-permute-start | bytes 49160 | tf_op jit(solution)/shard_map/ppermute | solution.py:19
  81.8 16.0 %collective-permute-start.14 = (f32[10,1,64]{2,1,0:T(1,128)S(1)}, f32[10,1,64]{2,1,0:T(1,128)S(1)}, u32[]{:S(2)}, u32[]{:S(2)}) collective-permute-start(f32[10,1,64]{2,1,0:T(1,128)S(1)} %get-tuple-element.80), channel_id=1, source_target_pairs={{1,0},{2,1},{3,2},{4,3},{5,4},{6,5},{7,6},{8,7},{9,8},{10,9},{11,1... | collective-permute-start | bytes 7688 | tf_op jit(solution)/shard_map/ppermute | solution.py:21
  87.9 10.0 %collective-permute-start.15 = (f32[10,1,64]{2,1,0:T(1,128)S(1)}, f32[10,1,64]{2,1,0:T(1,128)S(1)}, u32[]{:S(2)}, u32[]{:S(2)}) collective-permute-start(f32[10,1,64]{2,1,0:T(1,128)S(1)} %get-tuple-element.79), channel_id=1, source_target_pairs={{0,1},{1,2},{2,3},{3,4},{4,5},{5,6},{6,7},{7,8},{8,9},{9,10},{10,1... | collective-permute-start | bytes 7688 | tf_op jit(solution)/shard_map/ppermute | solution.py:19
  89.8 8.9 %collective-permute-start.10 = (f32[18,1,128]{2,1,0:T(1,128)S(1)}, f32[18,1,128]{2,1,0:T(1,128)S(1)}, u32[]{:S(2)}, u32[]{:S(2)}) collective-permute-start(f32[18,1,128]{2,1,0:T(1,128)S(1)} %get-tuple-element.60), channel_id=1, source_target_pairs={{1,0},{2,1},{3,2},{4,3},{5,4},{6,5},{7,6},{8,7},{9,8},{10,9},{11,1... | collective-permute-start | bytes 27656 | tf_op jit(solution)/shard_map/ppermute | solution.py:21
  95.9 7.7 %collective-permute-start.11 = (f32[18,1,128]{2,1,0:T(1,128)S(1)}, f32[18,1,128]{2,1,0:T(1,128)S(1)}, u32[]{:S(2)}, u32[]{:S(2)}) collective-permute-start(f32[18,1,128]{2,1,0:T(1,128)S(1)} %get-tuple-element.59), channel_id=1, source_target_pairs={{0,1},{1,2},{2,3},{3,4},{4,5},{5,6},{6,7},{7,8},{8,9},{9,10},{10,1... | collective-permute-start | bytes 27656 | tf_op jit(solution)/shard_map/ppermute | solution.py:19
  138.3 11.1 %collective-permute-start.18 = (f32[10,1,64]{2,1,0:T(1,128)S(1)}, f32[10,1,64]{2,1,0:T(1,128)S(1)}, u32[]{:S(2)}, u32[]{:S(2)}) collective-permute-start(f32[10,1,64]{2,1,0:T(1,128)S(1)} %get-tuple-element.78), channel_id=1, source_target_pairs={{1,0},{2,1},{3,2},{4,3},{5,4},{6,5},{7,6},{8,7},{9,8},{10,9},{11,1... | collective-permute-start | bytes 7688 | tf_op jit(solution)/shard_map/ppermute | solution.py:21
  140.2 9.1 %collective-permute-start.19 = (f32[10,1,64]{2,1,0:T(1,128)S(1)}, f32[10,1,64]{2,1,0:T(1,128)S(1)}, u32[]{:S(2)}, u32[]{:S(2)}) collective-permute-start(f32[10,1,64]{2,1,0:T(1,128)S(1)} %get-tuple-element.77), channel_id=1, source_target_pairs={{0,1},{1,2},{2,3},{3,4},{4,5},{5,6},{6,7},{7,8},{8,9},{9,10},{10,1... | collective-permute-start | bytes 7688 | tf_op jit(solution)/shard_map/ppermute | solution.py:19
  144.2 11.3 %collective-permute-start.24 = (f32[1,8,32]{2,1,0:T(8,128)S(1)}, f32[1,8,32]{2,1,0:T(8,128)S(1)}, u32[]{:S(2)}, u32[]{:S(2)}) collective-permute-start(f32[1,8,32]{2,1,0:T(8,128)S(1)} %get-tuple-element.104), channel_id=1, source_target_pairs={{64,0},{128,64},{192,128},{256,192},{320,256},{384,320},{448,384},... | collective-permute-start | bytes 3080 | tf_op jit(solution)/shard_map/ppermute | solution.py:21
  146.1 9.4 %collective-permute-start.25 = (f32[1,8,32]{2,1,0:T(8,128)S(1)}, f32[1,8,32]{2,1,0:T(8,128)S(1)}, u32[]{:S(2)}, u32[]{:S(2)}) collective-permute-start(f32[1,8,32]{2,1,0:T(8,128)S(1)} %get-tuple-element.103), channel_id=1, source_target_pairs={{0,64},{64,128},{128,192},{192,256},{256,320},{320,384},{384,448},... | collective-permute-start | bytes 3080 | tf_op jit(solution)/shard_map/ppermute | solution.py:19
  150.4 11.1 %collective-permute-start.20 = (f32[1,16,64]{2,1,0:T(8,128)S(1)}, f32[1,16,64]{2,1,0:T(8,128)S(1)}, u32[]{:S(2)}, u32[]{:S(2)}) collective-permute-start(f32[1,16,64]{2,1,0:T(8,128)S(1)} %get-tuple-element.84), channel_id=1, source_target_pairs={{64,0},{128,64},{192,128},{256,192},{320,256},{384,320},{448,384},... | collective-permute-start | bytes 12296 | tf_op jit(solution)/shard_map/ppermute | solution.py:21
  153.5 8.0 %collective-permute-start.21 = (f32[1,16,64]{2,1,0:T(8,128)S(1)}, f32[1,16,64]{2,1,0:T(8,128)S(1)}, u32[]{:S(2)}, u32[]{:S(2)}) collective-permute-start(f32[1,16,64]{2,1,0:T(8,128)S(1)} %get-tuple-element.83), channel_id=1, source_target_pairs={{0,64},{64,128},{128,192},{192,256},{256,320},{320,384},{384,448},... | collective-permute-start | bytes 12296 | tf_op jit(solution)/shard_map/ppermute | solution.py:19
  155.5 14.2 %collective-permute-start.26 = (f32[6,1,32]{2,1,0:T(1,128)S(1)}, f32[6,1,32]{2,1,0:T(1,128)S(1)}, u32[]{:S(2)}, u32[]{:S(2)}) collective-permute-start(f32[6,1,32]{2,1,0:T(1,128)S(1)} %get-tuple-element.96), channel_id=1, source_target_pairs={{1,0},{2,1},{3,2},{4,3},{5,4},{6,5},{7,6},{8,7},{9,8},{10,9},{11,1... | collective-permute-start | bytes 2312 | tf_op jit(solution)/shard_map/ppermute | solution.py:21
  159.6 10.1 %collective-permute-start.27 = (f32[6,1,32]{2,1,0:T(1,128)S(1)}, f32[6,1,32]{2,1,0:T(1,128)S(1)}, u32[]{:S(2)}, u32[]{:S(2)}) collective-permute-start(f32[6,1,32]{2,1,0:T(1,128)S(1)} %get-tuple-element.95), channel_id=1, source_target_pairs={{0,1},{1,2},{2,3},{3,4},{4,5},{5,6},{6,7},{7,8},{8,9},{9,10},{10,1... | collective-permute-start | bytes 2312 | tf_op jit(solution)/shard_map/ppermute | solution.py:19
  161.5 8.9 %collective-permute-start.22 = (f32[10,1,64]{2,1,0:T(1,128)S(1)}, f32[10,1,64]{2,1,0:T(1,128)S(1)}, u32[]{:S(2)}, u32[]{:S(2)}) collective-permute-start(f32[10,1,64]{2,1,0:T(1,128)S(1)} %get-tuple-element.76), channel_id=1, source_target_pairs={{1,0},{2,1},{3,2},{4,3},{5,4},{6,5},{7,6},{8,7},{9,8},{10,9},{11,1... | collective-permute-start | bytes 7688 | tf_op jit(solution)/shard_map/ppermute | solution.py:21
  167.6 7.6 %collective-permute-start.23 = (f32[10,1,64]{2,1,0:T(1,128)S(1)}, f32[10,1,64]{2,1,0:T(1,128)S(1)}, u32[]{:S(2)}, u32[]{:S(2)}) collective-permute-start(f32[10,1,64]{2,1,0:T(1,128)S(1)} %get-tuple-element.75), channel_id=1, source_target_pairs={{0,1},{1,2},{2,3},{3,4},{4,5},{5,6},{6,7},{7,8},{8,9},{9,10},{10,1... | collective-permute-start | bytes 7688 | tf_op jit(solution)/shard_map/ppermute | solution.py:19
  188.6 10.2 %collective-permute-start.30 = (f32[6,1,32]{2,1,0:T(1,128)S(1)}, f32[6,1,32]{2,1,0:T(1,128)S(1)}, u32[]{:S(2)}, u32[]{:S(2)}) collective-permute-start(f32[6,1,32]{2,1,0:T(1,128)S(1)} %get-tuple-element.94), channel_id=1, source_target_pairs={{1,0},{2,1},{3,2},{4,3},{5,4},{6,5},{7,6},{8,7},{9,8},{10,9},{11,1... | collective-permute-start | bytes 2312 | tf_op jit(solution)/shard_map/ppermute | solution.py:21
  190.5 8.3 %collective-permute-start.31 = (f32[6,1,32]{2,1,0:T(1,128)S(1)}, f32[6,1,32]{2,1,0:T(1,128)S(1)}, u32[]{:S(2)}, u32[]{:S(2)}) collective-permute-start(f32[6,1,32]{2,1,0:T(1,128)S(1)} %get-tuple-element.93), channel_id=1, source_target_pairs={{0,1},{1,2},{2,3},{3,4},{4,5},{5,6},{6,7},{7,8},{8,9},{9,10},{10,1... | collective-permute-start | bytes 2312 | tf_op jit(solution)/shard_map/ppermute | solution.py:19
  194.4 10.4 %collective-permute-start.36 = (f32[1,4,16]{2,1,0:T(4,128)S(1)}, f32[1,4,16]{2,1,0:T(4,128)S(1)}, u32[]{:S(2)}, u32[]{:S(2)}) collective-permute-start(f32[1,4,16]{2,1,0:T(4,128)S(1)} %get-tuple-element.122), channel_id=1, source_target_pairs={{64,0},{128,64},{192,128},{256,192},{320,256},{384,320},{448,384},... | collective-permute-start | bytes 776 | tf_op jit(solution)/shard_map/ppermute | solution.py:21
  196.4 8.5 %collective-permute-start.37 = (f32[1,4,16]{2,1,0:T(4,128)S(1)}, f32[1,4,16]{2,1,0:T(4,128)S(1)}, u32[]{:S(2)}, u32[]{:S(2)}) collective-permute-start(f32[1,4,16]{2,1,0:T(4,128)S(1)} %get-tuple-element.121), channel_id=1, source_target_pairs={{0,64},{64,128},{128,192},{192,256},{256,320},{320,384},{384,448},... | collective-permute-start | bytes 776 | tf_op jit(solution)/shard_map/ppermute | solution.py:19
  199.7 11.1 %collective-permute-start.32 = (f32[1,8,32]{2,1,0:T(8,128)S(1)}, f32[1,8,32]{2,1,0:T(8,128)S(1)}, u32[]{:S(2)}, u32[]{:S(2)}) collective-permute-start(f32[1,8,32]{2,1,0:T(8,128)S(1)} %get-tuple-element.100), channel_id=1, source_target_pairs={{64,0},{128,64},{192,128},{256,192},{320,256},{384,320},{448,384},... | collective-permute-start | bytes 3080 | tf_op jit(solution)/shard_map/ppermute | solution.py:21
  202.9 8.0 %collective-permute-start.33 = (f32[1,8,32]{2,1,0:T(8,128)S(1)}, f32[1,8,32]{2,1,0:T(8,128)S(1)}, u32[]{:S(2)}, u32[]{:S(2)}) collective-permute-start(f32[1,8,32]{2,1,0:T(8,128)S(1)} %get-tuple-element.99), channel_id=1, source_target_pairs={{0,64},{64,128},{128,192},{192,256},{256,320},{320,384},{384,448},... | collective-permute-start | bytes 3080 | tf_op jit(solution)/shard_map/ppermute | solution.py:19
  204.9 14.0 %collective-permute-start.38 = (f32[4,1,16]{2,1,0:T(1,128)S(1)}, f32[4,1,16]{2,1,0:T(1,128)S(1)}, u32[]{:S(2)}, u32[]{:S(2)}) collective-permute-start(f32[4,1,16]{2,1,0:T(1,128)S(1)} %get-tuple-element.112), channel_id=1, source_target_pairs={{1,0},{2,1},{3,2},{4,3},{5,4},{6,5},{7,6},{8,7},{9,8},{10,9},{11,1... | collective-permute-start | bytes 776 | tf_op jit(solution)/shard_map/ppermute | solution.py:21
  208.9 9.9 %collective-permute-start.39 = (f32[4,1,16]{2,1,0:T(1,128)S(1)}, f32[4,1,16]{2,1,0:T(1,128)S(1)}, u32[]{:S(2)}, u32[]{:S(2)}) collective-permute-start(f32[4,1,16]{2,1,0:T(1,128)S(1)} %get-tuple-element.111), channel_id=1, source_target_pairs={{0,1},{1,2},{2,3},{3,4},{4,5},{5,6},{6,7},{7,8},{8,9},{9,10},{10,1... | collective-permute-start | bytes 776 | tf_op jit(solution)/shard_map/ppermute | solution.py:19
  210.9 8.1 %collective-permute-start.34 = (f32[6,1,32]{2,1,0:T(1,128)S(1)}, f32[6,1,32]{2,1,0:T(1,128)S(1)}, u32[]{:S(2)}, u32[]{:S(2)}) collective-permute-start(f32[6,1,32]{2,1,0:T(1,128)S(1)} %get-tuple-element.92), channel_id=1, source_target_pairs={{1,0},{2,1},{3,2},{4,3},{5,4},{6,5},{7,6},{8,7},{9,8},{10,9},{11,1... | collective-permute-start | bytes 2312 | tf_op jit(solution)/shard_map/ppermute | solution.py:21
  216.9 7.6 %collective-permute-start.35 = (f32[6,1,32]{2,1,0:T(1,128)S(1)}, f32[6,1,32]{2,1,0:T(1,128)S(1)}, u32[]{:S(2)}, u32[]{:S(2)}) collective-permute-start(f32[6,1,32]{2,1,0:T(1,128)S(1)} %get-tuple-element.91), channel_id=1, source_target_pairs={{0,1},{1,2},{2,3},{3,4},{4,5},{5,6},{6,7},{7,8},{8,9},{9,10},{10,1... | collective-permute-start | bytes 2312 | tf_op jit(solution)/shard_map/ppermute | solution.py:19
  235.3 7.6 %collective-permute-start.43 = (f32[4,1,16]{2,1,0:T(1,128)S(1)}, f32[4,1,16]{2,1,0:T(1,128)S(1)}, u32[]{:S(2)}, u32[]{:S(2)}) collective-permute-start(f32[4,1,16]{2,1,0:T(1,128)S(1)} %get-tuple-element.109), channel_id=1, source_target_pairs={{0,1},{1,2},{2,3},{3,4},{4,5},{5,6},{6,7},{7,8},{8,9},{9,10},{10,1... | collective-permute-start | bytes 776 | tf_op jit(solution)/shard_map/ppermute | solution.py:19
  243.0 83.9 %collective-permute-start.44 = (f32[1,4,16]{2,1,0:T(4,128)S(1)}, f32[1,4,16]{2,1,0:T(4,128)S(1)}, u32[]{:S(2)}, u32[]{:S(2)}) collective-permute-start(f32[1,4,16]{2,1,0:T(4,128)S(1)} %get-tuple-element.118), channel_id=1, source_target_pairs={{64,0},{128,64},{192,128},{256,192},{320,256},{384,320},{448,384},... | collective-permute-start | bytes 776 | tf_op jit(solution)/shard_map/ppermute | solution.py:21
  245.0 82.0 %collective-permute-start.45 = (f32[1,4,16]{2,1,0:T(4,128)S(1)}, f32[1,4,16]{2,1,0:T(4,128)S(1)}, u32[]{:S(2)}, u32[]{:S(2)}) collective-permute-start(f32[1,4,16]{2,1,0:T(4,128)S(1)} %get-tuple-element.117), channel_id=1, source_target_pairs={{0,64},{64,128},{128,192},{192,256},{256,320},{320,384},{384,448},... | collective-permute-start | bytes 776 | tf_op jit(solution)/shard_map/ppermute | solution.py:19
  326.9 8.1 %collective-permute-start.46 = (f32[4,1,16]{2,1,0:T(1,128)S(1)}, f32[4,1,16]{2,1,0:T(1,128)S(1)}, u32[]{:S(2)}, u32[]{:S(2)}) collective-permute-start(f32[4,1,16]{2,1,0:T(1,128)S(1)} %get-tuple-element.108), channel_id=1, source_target_pairs={{1,0},{2,1},{3,2},{4,3},{5,4},{6,5},{7,6},{8,7},{9,8},{10,9},{11,1... | collective-permute-start | bytes 776 | tf_op jit(solution)/shard_map/ppermute | solution.py:21
  331.5 7.6 %collective-permute-start.47 = (f32[4,1,16]{2,1,0:T(1,128)S(1)}, f32[4,1,16]{2,1,0:T(1,128)S(1)}, u32[]{:S(2)}, u32[]{:S(2)}) collective-permute-start(f32[4,1,16]{2,1,0:T(1,128)S(1)} %get-tuple-element.107), channel_id=1, source_target_pairs={{0,1},{1,2},{2,3},{3,4},{4,5},{5,6},{6,7},{7,8},{8,9},{9,10},{10,1... | collective-permute-start | bytes 776 | tf_op jit(solution)/shard_map/ppermute | solution.py:19
  340.1 18.8 %all-to-all-start = ((f32[64,1,128]{2,1,0:T(1,128)}), f32[64,1,128]{2,1,0:T(1,128)S(1)}, u32[]{:S(2)}, u32[]{:S(2)}) async-start(f32[64,1,128]{2,1,0:T(1,128)} %reshape.107), calls=%async_computation | async-start | bytes 65536 | tf_op jit(solution)/shard_map/all_to_all | solution.py:133
  345.6 20.5 %collective-permute-start.48 = (f32[1,128,8]{1,2,0:T(8,128)S(1)}, f32[1,128,8]{1,2,0:T(8,128)S(1)}, u32[]{:S(2)}, u32[]{:S(2)}) collective-permute-start(f32[1,128,8]{1,2,0:T(8,128)S(1)} %multiply_bitcast_fusion), channel_id=1, source_target_pairs={{64,0},{128,64},{192,128},{256,192},{320,256},{384,320},{448,384},... | collective-permute-start | bytes 12296 | tf_op jit(solution)/shard_map/ppermute | solution.py:21
  347.5 18.6 %collective-permute-start.50 = (f32[1,128,8]{1,2,0:T(8,128)S(1)}, f32[1,128,8]{1,2,0:T(8,128)S(1)}, u32[]{:S(2)}, u32[]{:S(2)}) collective-permute-start(f32[1,128,8]{1,2,0:T(8,128)S(1)} %multiply_bitcast_fusion), channel_id=1, source_target_pairs={{0,64},{64,128},{128,192},{192,256},{256,320},{320,384},{384,448},... | collective-permute-start | bytes 12296 | tf_op jit(solution)/shard_map/ppermute | solution.py:19
  420.7 6.6 %collective-permute-start.54 = (f32[1,128,8]{1,2,0:T(8,128)S(1)}, f32[1,128,8]{1,2,0:T(8,128)S(1)}, u32[]{:S(2)}, u32[]{:S(2)}) collective-permute-start(f32[1,128,8]{1,2,0:T(8,128)S(1)} %multiply_add_fusion.2), channel_id=1, source_target_pairs={{64,0},{128,64},{192,128},{256,192},{320,256},{384,320},{448,384},... | collective-permute-start | bytes 12296 | tf_op jit(solution)/shard_map/ppermute | solution.py:21
  479.8 6.6 %collective-permute-start.58 = (f32[1,128,8]{1,2,0:T(8,128)S(1)}, f32[1,128,8]{1,2,0:T(8,128)S(1)}, u32[]{:S(2)}, u32[]{:S(2)}) collective-permute-start(f32[1,128,8]{1,2,0:T(8,128)S(1)} %multiply_add_fusion.1), channel_id=1, source_target_pairs={{64,0},{128,64},{192,128},{256,192},{320,256},{384,320},{448,384},... | collective-permute-start | bytes 12296 | tf_op jit(solution)/shard_map/ppermute | solution.py:21
  539.3 6.6 %collective-permute-start.62 = (f32[1,128,8]{1,2,0:T(8,128)S(1)}, f32[1,128,8]{1,2,0:T(8,128)S(1)}, u32[]{:S(2)}, u32[]{:S(2)}) collective-permute-start(f32[1,128,8]{1,2,0:T(8,128)S(1)} %multiply_add_fusion), channel_id=1, source_target_pairs={{64,0},{128,64},{192,128},{256,192},{320,256},{384,320},{448,384},... | collective-permute-start | bytes 12296 | tf_op jit(solution)/shard_map/ppermute | solution.py:21
  595.1 7.6 %collective-permute-start.69 = (f32[4,1,16]{2,1,0:T(1,128)S(1)}, f32[4,1,16]{2,1,0:T(1,128)S(1)}, u32[]{:S(2)}, u32[]{:S(2)}) collective-permute-start(f32[4,1,16]{2,1,0:T(1,128)S(1)} %get-tuple-element.105), channel_id=1, source_target_pairs={{0,1},{1,2},{2,3},{3,4},{4,5},{5,6},{6,7},{7,8},{8,9},{9,10},{10,1... | collective-permute-start | bytes 776 | tf_op jit(solution)/shard_map/ppermute | solution.py:19
  610.7 6.1 collective-permute-start.72
  612.6 7.6 %collective-permute-start.73 = (f32[6,1,32]{2,1,0:T(1,128)S(1)}, f32[6,1,32]{2,1,0:T(1,128)S(1)}, u32[]{:S(2)}, u32[]{:S(2)}) collective-permute-start(f32[6,1,32]{2,1,0:T(1,128)S(1)} %get-tuple-element.89), channel_id=1, source_target_pairs={{0,1},{1,2},{2,3},{3,4},{4,5},{5,6},{6,7},{7,8},{8,9},{9,10},{10,1... | collective-permute-start | bytes 2312 | tf_op jit(solution)/shard_map/ppermute | solution.py:19
  630.4 7.6 %collective-permute-start.77 = (f32[10,1,64]{2,1,0:T(1,128)S(1)}, f32[10,1,64]{2,1,0:T(1,128)S(1)}, u32[]{:S(2)}, u32[]{:S(2)}) collective-permute-start(f32[10,1,64]{2,1,0:T(1,128)S(1)} %get-tuple-element.73), channel_id=1, source_target_pairs={{0,1},{1,2},{2,3},{3,4},{4,5},{5,6},{6,7},{7,8},{8,9},{9,10},{10,1... | collective-permute-start | bytes 7688 | tf_op jit(solution)/shard_map/ppermute | solution.py:19
  650.9 7.7 %collective-permute-start.81 = (f32[18,1,128]{2,1,0:T(1,128)S(1)}, f32[18,1,128]{2,1,0:T(1,128)S(1)}, u32[]{:S(2)}, u32[]{:S(2)}) collective-permute-start(f32[18,1,128]{2,1,0:T(1,128)S(1)} %get-tuple-element.57), channel_id=1, source_target_pairs={{0,1},{1,2},{2,3},{3,4},{4,5},{5,6},{6,7},{7,8},{8,9},{9,10},{10,1... | collective-permute-start | bytes 27656 | tf_op jit(solution)/shard_map/ppermute | solution.py:19
  (69 other events, 3399.3 us)
